TPU v7x, 256 devices: a whole 4x4x8 slice. The times are simulated.
256 devices in a mesh: dp: 64 (over x, z, core), mp: 4 (over y).
Axes of the slice: x: 4, y: 4, z: 8, core: 2. Of those that a mesh axis runs over, the one named last changes fastest.
Arguments:
- activations: bfloat16 [32768, 2560], P('dp'), may hold values from -6 to 6
- cotangent: bfloat16 [32768, 6912], P('dp', 'mp'), may hold values from -6 to 6
- frozen_weight: bfloat16 [2560, 6912], P(None, 'mp'), may hold values from -0.078125 to 0.078125
- skew_params: bfloat16 [10, 256, 256], replicated, may hold values from -0.125 to 0.125
- tile_order: int32 [20], replicated, may hold values from 0 to 19, each once
- block_owner: int32 [10], replicated, may hold values from 0 to 63, as said below
Outputs:
- input_grad: bfloat16 [32768, 2560], P('dp', 'mp')
- skew_grads: float32 [192, 256, 256], P('dp')
Inputs may be any that keep to these rules, and one draw needn't show every extreme that they name: `tile_order`: a permutation of the 20 tiles. `block_owner`: no index of dp owns more than 3 blocks, and some index owns exactly 3; indices 0 and 64 - 1 own blocks in every draw.
All inputs are finite; a program needn't handle non-finite values.
Results may differ from a plain program's by a relative error of at most 0.001.
Values sent between devices are 32-bit elements; how exact they have to be, the bound alone decides.
No kernel may reach another device: no remote copies, remote signals or barrier semaphores. Data moves between devices by JAX's collectives and lax.ppermute only.
A program may use at most 128 MiB of HBM per device.

v0:
```python
import math
import jax
import jax.numpy as jnp
from jax import lax
from jax.sharding import PartitionSpec as P

SLOTS = 3
highest = lax.Precision.HIGHEST


def product(first, second):
    return jnp.einsum("bij,bjk->bik", first, second, precision=highest)


def cayley_parts(params):
    plain = params.astype(jnp.float32)
    skew = plain - jnp.swapaxes(plain, 1, 2)
    square = product(skew, skew)
    cube = product(square, skew)
    identity = jnp.eye(skew.shape[1], dtype=jnp.float32)
    return (skew, identity[None] + 2.0 * skew + 2.0 * square + cube)


def to_blocks(matrix, order, tile_count, block_count):
    tiled = matrix.reshape(matrix.shape[0], tile_count, -1)
    return jnp.take(tiled, order, axis=1).reshape(matrix.shape[0], block_count, -1)


def inverse_order(order, tile_count):
    positions = jnp.arange(tile_count, dtype=jnp.int32)
    matches = (order[:, None] == positions[None, :]).astype(jnp.int32)
    return jnp.sum(positions[:, None] * matches, axis=0)


def adjoint(gram, skew):
    transposed = jnp.swapaxes(skew, 1, 2)
    left = product(gram, transposed)
    right = product(transposed, gram)
    total = (
        2.0 * gram
        + 2.0 * (left + right)
        + product(left, transposed)
        + product(transposed, left)
        + product(transposed, right)
    )
    return total - jnp.swapaxes(total, 1, 2)


def local(activations, cotangent, frozen_weight, skew_params, tile_order, block_owner):
    token_rows = activations.shape[0]
    tile_count = tile_order.shape[0]
    block_count = block_owner.shape[0]
    skew, rotation = cayley_parts(skew_params)
    partial_grad = lax.dot_general(
        cotangent, frozen_weight, (((1,), (1,)), ((), ())), preferred_element_type=jnp.float32
    )
    feature_grad = lax.psum(partial_grad, "mp")
    grad_blocks = to_blocks(feature_grad, tile_order, tile_count, block_count)
    own_tiles = tile_count // lax.axis_size("mp")
    inverse = inverse_order(tile_order, tile_count)
    own_places = lax.dynamic_slice_in_dim(inverse, lax.axis_index("mp") * own_tiles, own_tiles, 0)
    half_rows = rotation.reshape(block_count * 2, rotation.shape[1] // 2, rotation.shape[2])
    own_rotation = jnp.take(half_rows, own_places, axis=0)
    own_blocks = jnp.take(grad_blocks, own_places // 2, axis=1)
    own_rotated = jnp.einsum("tkj,kij->tki", own_blocks, own_rotation, precision=highest)
    input_grad = own_rotated.reshape(token_rows, -1).astype(jnp.bfloat16)
    quarter = token_rows // lax.axis_size("mp")
    row_start = lax.axis_index("mp") * quarter
    some_inputs = lax.dynamic_slice_in_dim(activations, row_start, quarter, 0)
    input_blocks = to_blocks(some_inputs, tile_order, tile_count, block_count).astype(jnp.float32)
    some_grads = lax.dynamic_slice_in_dim(grad_blocks, row_start, quarter, 0)
    local_gram = jnp.einsum("tbi,tbj->bij", input_blocks, some_grads, precision=highest)
    gram = lax.psum(local_gram, ("dp", "mp"))
    owned = (block_owner == lax.axis_index("dp")).astype(jnp.int32)
    ranking = jnp.cumsum(owned) - 1
    slot_ids = jnp.arange(SLOTS, dtype=jnp.int32)
    selector = ((owned[None, :] == 1) & (ranking[None, :] == slot_ids[:, None])).astype(jnp.float32)
    gram_slots = jnp.einsum("sb,bij->sij", selector, gram, precision=highest)
    skew_slots = jnp.einsum("sb,bij->sij", selector, skew, precision=highest)
    scaling = 1.0 / math.sqrt(token_rows * lax.axis_size("dp"))
    skew_grads = adjoint(gram_slots, skew_slots) * scaling
    return (input_grad, skew_grads)


def solution(mesh):
    placed = (P("dp", None), P("dp", "mp"), P(None, "mp"), P(), P(), P())
    return jax.shard_map(
        local,
        mesh=mesh,
        in_specs=placed,
        out_specs=(P("dp", "mp"), P("dp", None, None)),
        check_vma=False,
    )
```

profile of v0, /device:TPU:2, one launch (start us, length us, event | category | flops | bytes accessed | tf_op | source)
XLA Modules:
  0.0 453.6 jit_solution(274264501818761207)
XLA Ops:
  7.2 11.4 %fusion.34 = f32[512,2560]{0,1:T(8,128)} fusion(bf16[512,1728]{0,1:T(8,128)(2,1)} %param.7, bf16[2560,1728]{0,1:T(8,128)(2,1)} %param.8), kind=kOutput, calls=%fused_computation.62 | convolution fusion | flops 4529848320 | bytes 15859712 | tf_op jit(solution)/shard_map/dot_general | solution.py:54
  18.7 5.9 %copy.80 = f32[512,20,128]{2,0,1:T(8,128)} copy(f32[512,20,128]{0,2,1:T(8,128)} %bitcast.49) | data formatting | bytes 10485760 | tf_op jit(solution)/shard_map/reshape | solution.py:25
  27.4 1.6 copy.77
  29.1 1.9 copy.78
  31.7 2.4 bitcast_subtract_fusion
  34.1 3.9 fusion
  38.0 104.7 %all-reduce.3.cloned.1.call-done = f32[512,20,128]{2,0,1:T(8,128)} async-done(((f32[512,20,128]{2,0,1:T(8,128)}), f32[512,20,128]{2,0,1:T(8,128)}) %all-reduce.3.cloned.1.call-update) | async-done | bytes 5242896 | tf_op jit(solution)/shard_map/psum | solution.py:57
  142.7 5.7 %gather_fusion.1 = f32[20,512,128]{2,1,0:T(8,128)} fusion(f32[512,20,128]{2,0,1:T(8,128)} %all-reduce.3.cloned.1.call-done, s32[1024]{0:T(1024)S(1)} %pad_clamp_fusion.1), kind=kCustom, calls=%fused_computation.1 | custom fusion | bytes 10485840 | tf_op jit(solution)/shard_map/jit(_take)/gather | solution.py:26
  148.4 5.9 %copy.81 = f32[512,20,128]{0,2,1:T(8,128)} copy(f32[512,20,128]{2,0,1:T(8,128)} %bitcast.47) | data formatting | bytes 10485760 | tf_op jit(solution)/shard_map/jit(_take)/gather | solution.py:26
  154.3 5.9 %copy.82 = f32[512,10,256]{2,0,1:T(8,128)} copy(f32[512,10,256]{0,2,1:T(8,128)} %bitcast.48) | data formatting | bytes 10485760 | tf_op jit(solution)/shard_map/jit(_take)/gather | solution.py:26
  160.2 2.9 broadcast_select_fusion
  163.1 2.3 copy-done.2
  165.4 2.8 fusion.11
  168.3 1.5 copy.90
  169.8 2.9 fusion.33
  172.7 4.8 %add_add_fusion = f32[10,256,256]{2,1,0:T(8,128)} fusion(f32[10,256,256]{2,1,0:T(8,128)S(1)} %fusion.33, f32[10,256,256]{2,1,0:T(8,128)S(1)} %bitcast_subtract_fusion, f32[256,256]{1,0:T(8,128)S(1)} %fusion.24), kind=kOutput, calls=%fused_computation.13 | convolution fusion | flops 2016542720 | bytes 8126464 | tf_op jit(solution)/shard_map/bij,bjk->bik/dot_general | solution.py:12
  177.4 3.2 gather_fusion
  180.6 3.2 gather_fusion.2
  183.8 4.7 %fusion.7 = bf16[5,128,512]{2,1,0:T(8,128)(2,1)} fusion(f32[5,512,256]{2,1,0:T(8,128)S(1)} %gather_fusion.2, pred[5]{0:T(512)(128)(4,1)S(1)} %get-tuple-element.16, f32[5,128,256]{2,1,0:T(8,128)} %gather_fusion, pred[5]{0:T(512)(128)(4,1)S(1)} %get-tuple-element.10), kind=kOutput, calls=%fused_computation.14 | convolution fusion | flops 1007779840 | bytes 3932170 | tf_op jit(solution)/shard_map/tkj,kij->tki/dot_general | solution.py:65
  188.5 2.2 copy.97
  190.7 240.4 %all-reduce.5.cloned.1.call-done = f32[10,256,256]{2,1,0:T(8,128)} async-done(((f32[10,256,256]{2,1,0:T(8,128)}), f32[10,256,256]{2,1,0:T(8,128)}) %all-reduce.5.cloned.1.call-update) | async-done | bytes 2621456 | tf_op jit(solution)/shard_map/psum | solution.py:73
  431.1 4.8 %fusion.2 = f32[3,256,256]{2,0,1:T(4,128)S(1)} fusion(f32[10,256,256]{2,1,0:T(8,128)} %all-reduce.5.cloned.1.call-done, s32[10]{0:T(128)S(1)} %add_bitcast_fusion, pred[10]{0:T(512)(128)(4,1)S(1)} %get-tuple-element.14), kind=kOutput, calls=%fused_computation.6 | convolution fusion | flops 23593020 | bytes 3407922 | tf_op jit(solution)/shard_map/sb,bij->sij/dot_general | solution.py:78
  440.1 1.8 convolution_add_fusion
  441.9 2.3 copy.96
  (43 shorter events, 10.2 us)
Async XLA Ops:
  7.2 18.5 %copy-start = (bf16[512,2560]{1,0:T(8,128)(2,1)S(1)}, bf16[512,2560]{1,0:T(8,128)(2,1)}, u32[]{:S(2)}) copy-start(bf16[512,2560]{1,0:T(8,128)(2,1)} %param.6) | copy-start | bytes 7864324
  7.2 135.6 %all-reduce.3.cloned.1.call-start = ((), (), s32[]{:S(2)}) async-start(), calls=%async_computation | async-start | bytes 10485760 | tf_op jit(solution)/shard_map/psum | solution.py:57
  24.6 0.7 copy-start.5
  24.6 0.8 copy-start.6
  24.6 406.5 %all-reduce.5.cloned.1.call-start = ((), (), s32[]{:S(2)}) async-start(), calls=%async_computation.1 | async-start | bytes 5242880 | tf_op jit(solution)/shard_map/psum | solution.py:73
  29.0 2.1 copy-start.4
  163.1 2.3 copy-start.2
  190.7 245.2 %copy-start.3 = (f32[3,256,256]{2,0,1:T(4,128)S(1)}, f32[3,256,256]{2,0,1:T(4,128)}, u32[]{:S(2)}) copy-start(f32[3,256,256]{2,0,1:T(4,128)} %fusion) | copy-start | bytes 2359300
  440.1 6.7 %copy-start.1 = (bf16[512,2560]{1,0:T(8,128)(2,1)S(1)}, bf16[512,2560]{1,0:T(8,128)(2,1)}, u32[]{:S(2)}) copy-start(bf16[512,2560]{1,0:T(8,128)(2,1)} %param.6) | copy-start | bytes 7864324
Sparse Core Ops, SparseCore 0:
  24.7 117.9 all-reduce.2
  168.4 262.7 all-reduce.4
where the time goes:
time: 454 us
  waiting for transfers between devices  345 us (76%)
  local copies, waits for them, and re-layouts  45.2 us (10%)
  matrix products  41.2 us (9%)
  between operations  14.3 us (3%)
  other arithmetic  7.66 us (2%)
    psum x1, waiting for transfers between devices, local(): gram = lax.psum(local_gram, ('dp', 'mp'))  240 us
    psum x1, waiting for transfers between devices, local(): feature_grad = lax.psum(partial_grad, 'mp')  105 us
    gather x5, local copies, waits for them, and re-layouts, to_blocks(): jnp.take(tiled, order, axis=1).reshape(matrix.shape[0], block_count, -1)  18.5 us
    dot_general x7, matrix products, product(): return jnp.einsum('bij,bjk->bik', first, second, precision=highest)  13.5 us
    dot_general x1, matrix products, local(): lax.dot_general(cotangent, frozen_weight, (((1,), (1,)), ((), ())), prefe...  11.4 us
  transfers between devices with their start and end apart: 2, of which 2 were waited for; matrix products, arithmetic and copies ran while one was open for 8% of the time, Pallas kernels for 0%

commit v1 on v0

--- a/solution.py
+++ b/solution.py
@@ -6,6 +6,11 @@
 
 SLOTS = 3
 highest = lax.Precision.HIGHEST
+
+
+def gather_and_add(x, axis):
+    parts = lax.all_gather(x, axis)
+    return jnp.sum(parts, axis=0)
 
 
 def product(first, second):
@@ -54,7 +59,7 @@
     partial_grad = lax.dot_general(
         cotangent, frozen_weight, (((1,), (1,)), ((), ())), preferred_element_type=jnp.float32
     )
-    feature_grad = lax.psum(partial_grad, "mp")
+    feature_grad = gather_and_add(partial_grad, "mp")
     grad_blocks = to_blocks(feature_grad, tile_order, tile_count, block_count)
     own_tiles = tile_count // lax.axis_size("mp")
     inverse = inverse_order(tile_order, tile_count)

time: 454 us -> 549 us (1.21)
  waiting for transfers between devices: 345 us -> 421 us
  other arithmetic: 7.66 us -> 18.9 us
  local copies, waits for them, and re-layouts: 45.2 us -> 52.7 us
    all_gather x0 -> x1, waiting for transfers between devices: none -> 180 us  [gather_and_add(): parts = lax.all_gather(x, axis)]
    psum x1 -> x0, waiting for transfers between devices: 105 us -> none  [local(): feature_grad = lax.psum(partial_grad, 'mp')]
    reduce_sum x0 -> x1, other arithmetic: none -> 11.2 us  [gather_and_add(): return jnp.sum(parts, axis=0)]
    reduce_sum x0 -> x1, local copies, waits for them, and re-layouts: none -> 5.9 us  [gather_and_add(): return jnp.sum(parts, axis=0)]
  transfers between devices with their start and end apart: 2 -> 2, of which waited for: 2 -> 2; matrix products, arithmetic and copies ran while one was open for 8% -> 7% of each run, Pallas kernels for 0% -> 0%
where the time goes in v1:
time: 549 us; the launch traced here: 548 us
  waiting for transfers between devices  421 us (77%)
  local copies, waits for them, and re-layouts  52.7 us (10%)
  matrix products  41.2 us (8%)
  other arithmetic  18.9 us (3%)
  between operations  14.3 us (3%)
    psum x1, waiting for transfers between devices, local(): gram = lax.psum(local_gram, ('dp', 'mp'))  241 us
    all_gather x1, waiting for transfers between devices, gather_and_add(): parts = lax.all_gather(x, axis)  180 us
    gather x5, local copies, waits for them, and re-layouts, to_blocks(): jnp.take(tiled, order, axis=1).reshape(matrix.shape[0], block_count, -1)  18.5 us
    dot_general x7, matrix products, product(): return jnp.einsum('bij,bjk->bik', first, second, precision=highest)  13.5 us
    dot_general x1, matrix products, local(): lax.dot_general(cotangent, frozen_weight, (((1,), (1,)), ((), ())), prefe...  11.5 us
    reduce_sum x1, other arithmetic, gather_and_add(): return jnp.sum(parts, axis=0)  11.2 us
  transfers between devices with their start and end apart: 2, of which 2 were waited for; matrix products, arithmetic and copies ran while one was open for 7% of the time, Pallas kernels for 0%

profile of v1, /device:TPU:2, one launch (start us, length us, event | category | flops | bytes accessed | tf_op | source)
XLA Modules:
  0.0 548.5 jit_solution(5337816072456594659)
XLA Ops:
  7.2 11.5 %fusion.34 = f32[512,2560]{1,0:T(8,128)} fusion(bf16[512,1728]{0,1:T(8,128)(2,1)} %param.7, bf16[2560,1728]{0,1:T(8,128)(2,1)} %param.8), kind=kOutput, calls=%fused_computation.62 | convolution fusion | flops 4529848320 | bytes 15859712 | tf_op jit(solution)/shard_map/dot_general | solution.py:59
  19.6 2.5 copy.102
  22.1 2.8 copy.103
  27.5 2.4 bitcast_subtract_fusion
  29.9 3.9 fusion
  33.8 180.2 %all-gather.3.cloned.1.call-done = f32[2048,2560]{1,0:T(8,128)} async-done(((f32[512,2560]{1,0:T(8,128)}), f32[2048,2560]{1,0:T(8,128)}) %all-gather.3.cloned.1.call-update) | async-done | bytes 20971536 | tf_op jit(solution)/shard_map/all_gather | solution.py:12
  214.0 11.2 %reduce_sum.19 = f32[512,2560]{1,0:T(8,128)} reduce(f32[4,512,2560]{2,1,0:T(8,128)} %bitcast.49, f32[]{:T(128)} %constant.92.clone.1), dimensions={0}, to_apply=%region_1.2 | reduce | flops 3932160 | bytes 26214404 | tf_op jit(solution)/shard_map/reduce_sum | solution.py:13
  225.2 5.9 %copy.104 = f32[512,2560]{0,1:T(8,128)} copy(f32[512,2560]{1,0:T(8,128)} %reduce_sum.19) | data formatting | bytes 10485760 | tf_op jit(solution)/shard_map/reduce_sum | solution.py:13
  231.1 5.9 %copy.105 = f32[512,20,128]{2,0,1:T(8,128)} copy(f32[512,20,128]{0,2,1:T(8,128)} %bitcast.50) | data formatting | bytes 10485760 | tf_op jit(solution)/shard_map/reshape | solution.py:30
  237.0 5.7 %gather_fusion.1 = f32[20,512,128]{2,1,0:T(8,128)} fusion(f32[512,20,128]{2,0,1:T(8,128)} %copy.105, s32[1024]{0:T(1024)S(1)} %pad_clamp_fusion.1), kind=kCustom, calls=%fused_computation.1 | custom fusion | bytes 10485840 | tf_op jit(solution)/shard_map/jit(_take)/gather | solution.py:31
  242.7 5.9 %copy.106 = f32[512,20,128]{0,2,1:T(8,128)} copy(f32[512,20,128]{2,0,1:T(8,128)} %bitcast.48) | data formatting | bytes 10485760 | tf_op jit(solution)/shard_map/jit(_take)/gather | solution.py:31
  248.6 5.9 %copy.107 = f32[512,10,256]{2,0,1:T(8,128)} copy(f32[512,10,256]{0,2,1:T(8,128)} %bitcast.51) | data formatting | bytes 10485760 | tf_op jit(solution)/shard_map/jit(_take)/gather | solution.py:31
  254.6 2.9 broadcast_select_fusion
  257.5 2.3 copy-done.2
  259.8 2.8 fusion.11
  264.1 2.9 fusion.33
  267.0 4.8 add_add_fusion
  271.8 3.2 gather_fusion
  274.9 3.2 gather_fusion.2
  278.1 4.7 fusion.7
  282.9 2.2 copy.122
  285.0 240.9 %all-reduce.2.cloned.1.call-done = f32[10,256,256]{2,1,0:T(8,128)} async-done(((f32[10,256,256]{2,1,0:T(8,128)}), f32[10,256,256]{2,1,0:T(8,128)}) %all-reduce.2.cloned.1.call-update) | async-done | bytes 2621456 | tf_op jit(solution)/shard_map/psum | solution.py:78
  525.9 4.8 fusion.2
  536.7 2.3 copy.121
  (43 shorter events, 13.5 us)
Async XLA Ops:
  7.2 17.9 %copy-start = (bf16[512,2560]{1,0:T(8,128)(2,1)S(1)}, bf16[512,2560]{1,0:T(8,128)(2,1)}, u32[]{:S(2)}) copy-start(bf16[512,2560]{1,0:T(8,128)(2,1)} %param.6) | copy-start | bytes 7864324
  7.2 206.8 %all-gather.3.cloned.1.call-start = ((), (), s32[]{:S(2)}) async-start(), calls=%async_computation.1 | async-start | bytes 26214400 | tf_op jit(solution)/shard_map/all_gather | solution.py:12
  18.7 0.7 copy-start.5
  18.7 507.2 %all-reduce.2.cloned.1.call-start = ((), (), s32[]{:S(2)}) async-start(), calls=%async_computation | async-start | bytes 5242880 | tf_op jit(solution)/shard_map/psum | solution.py:78
  22.1 2.8 copy-start.4
  257.5 2.3 copy-start.2
  285.0 245.8 %copy-start.3 = (f32[3,256,256]{2,0,1:T(4,128)S(1)}, f32[3,256,256]{2,0,1:T(4,128)}, u32[]{:S(2)}) copy-start(f32[3,256,256]{2,0,1:T(4,128)} %fusion) | copy-start | bytes 2359300
  534.9 6.7 %copy-start.1 = (bf16[512,2560]{1,0:T(8,128)(2,1)S(1)}, bf16[512,2560]{1,0:T(8,128)(2,1)}, u32[]{:S(2)}) copy-start(bf16[512,2560]{1,0:T(8,128)(2,1)} %param.6) | copy-start | bytes 7864324
Sparse Core Ops, SparseCore 0:
  18.9 195.0 all-gather.2
  262.7 263.1 all-reduce.1
